TPU v7x, 128 devices: a whole 4x4x4 slice. The times are simulated.
128 devices in a mesh: row: 8 (over y, core), col: 16 (over z, x).
Axes of the slice: x: 4, y: 4, z: 4, core: 2. Of those that a mesh axis runs over, the one named last changes fastest.
Arguments:
- pattern: int32 [16, 32, 9], P('row', 'col'), may hold values from 0 to 1, as said below
- start: float32 [16, 32, 9, 128, 128], P('row', 'col'), may hold values from -1 to 1, as said below
Outputs:
- sign_estimate: float32 [16, 32, 9, 128, 128], P('row', 'col')
Inputs may be any that keep to these rules, and one draw needn't show every extreme that they name: Offset 4 (the site itself) is always 1; the pattern is symmetric: pattern[p, k] = pattern[p + step(k), 8 - k], and 0 where the neighbour lies outside the grid; about 8 ones a site. Symmetric: start[p, k] is the transpose of start[p + step(k), 8 - k] wherever that neighbour lies in the grid.
All inputs are finite; a program needn't handle non-finite values.
Results may differ from a plain program's by a relative error of at most 0.0001.
Values sent between devices are 32-bit elements; how exact they have to be, the bound alone decides.
A program may use at most 320 MiB of HBM per device.

v0:
```python
import functools

import jax
import jax.numpy as jnp
from jax import lax
from jax.experimental import pallas as pl
from jax.experimental.pallas import tpu as pltpu
from jax.sharding import PartitionSpec as P

MESH = pl.DeviceIdType.MESH
SIDES = ((0, 1), (0, -1), (1, 0), (-1, 0))
INNER = (((0, 0), ((0, 0), (0, -1))), ((0, 0), ((-1, 0), (-1, -1))))
OUTER = (
    ((0, 0), ((1, 1), (1, 0))),
    ((0, 0), ((0, 1), (-1, 1))),
    ((0, 0), ((1, -1),)),
)
RING = (
    ((1, 0), ((0, 0), (0, -1))),
    ((0, 1), ((0, 0), (-1, 0))),
    ((1, 1), ((0, 0),)),
)
OUTSIDE = ((1, 1), (1, 0), (1, -1), (0, 1), (-1, 1))


def near(p, q):
    return abs(p[0] - q[0]) <= 1 and abs(p[1] - q[1]) <= 1


def offset(dr, dc):
    return (dr + 1) * 3 + dc + 1


class Corner:
    def __init__(self, n):
        self.a, self.b = 1 + n // 2, 1 + lax.rem(n, 2)
        self.down, self.across = 2 * self.a - 3, 2 * self.b - 3

    def at(self, src, dst):
        i = self.a + src[0] * self.down
        j = self.b + src[1] * self.across
        return i, j, offset((dst[0] - src[0]) * self.down, (dst[1] - src[1]) * self.across)

    def index(self, src, dst):
        i, j, k = self.at(src, dst)
        return i * 4 + j, k

    def get(self, ref, src, dst):
        return ref[self.index(src, dst)]

    def keep(self, pat, src, dst):
        if max(src) == 1:
            src, dst = dst, src
        i, j, k = self.at(src, dst)
        return pat[i - 1, j - 1, k].astype(jnp.float32)


def sends(symmetric):
    plan = {}
    for side in SIDES:
        if side[0] == 0:
            c = 2 if side[1] == 1 else 1
            first = [((1, c), (1, c)), ((2, c), (2, c)), ((1, c), (2, c))]
            later = [((1, c), (0, c)), ((2, c), (3, c))]
            relay = []
        else:
            r = 2 if side[0] == 1 else 1
            o = r + side[0]
            first = [((r, 1), (r, 1)), ((r, 2), (r, 2)), ((r, 1), (r, 2))]
            later = [((r, 1), (r, 0)), ((r, 2), (r, 3)), ((r, 1), (o, 0)), ((r, 2), (o, 3))]
            relay = [((r, 0), (r, 0)), ((r, 3), (r, 3))]
        if not symmetric:
            first = first + [(q, p) for p, q in first if p != q]
            later = later + [(q, p) for p, q in later]
        plan[side] = (first, later, relay)
    return plan


def kernel(rows, cols, pat, start, out, x0, s0, x1, s1, send_sem, recv_sem):
    row, col = lax.axis_index("row"), lax.axis_index("col")
    block = start.shape[-1]

    def device(side):
        return (lax.rem(row + side[0] + rows, rows), lax.rem(col + side[1] + cols, cols))

    barrier = pltpu.get_barrier_semaphore()
    for side in SIDES:
        pl.semaphore_signal(barrier, inc=1, device_id=device(side), device_id_type=MESH)

    def copies(phase, group, sides=SIDES):
        table = tables[phase]
        result = []
        for d, side in enumerate(SIDES):
            if side not in sides:
                continue
            groups = sends(phase < 2)[side]
            base = sum(len(g) for g in groups[:group])
            for n, (p, q) in enumerate(groups[group]):
                k = offset(q[0] - p[0], q[1] - p[1])
                here = p[0] * 4 + p[1]
                there = here - 2 * (side[0] * 4 + side[1])
                result.append(
                    pltpu.make_async_remote_copy(
                        src_ref=table.at[here, k],
                        dst_ref=table.at[there, k],
                        send_sem=send_sem.at[phase, d, base + n],
                        recv_sem=recv_sem.at[phase, d, base + n],
                        device_id=device(side),
                        device_id_type=MESH,
                    )
                )
        return result

    tables = (x0, s0, x1, s1)

    def begin(phase, group):
        for c in copies(phase, group):
            c.start()

    def arrive(phase, group, sides=SIDES):
        for c in copies(phase, group, sides):
            c.wait_recv()

    def pass_on(phase):
        arrive(phase, 0, SIDES[:2])
        begin(phase, 2)

    def settle(phase):
        arrive(phase, 0, SIDES[2:])
        arrive(phase, 1)
        arrive(phase, 2)

    def corners(body):
        def step(n, carry):
            body(Corner(n))
            return carry

        lax.fori_loop(0, 4, step, 0)

    def product(left, right, groups, emit):
        zero = jnp.zeros((block, block), jnp.float32)

        def body(c):
            for src, dsts in groups:
                mids = [
                    (i, j)
                    for i in (-1, 0, 1)
                    for j in (-1, 0, 1)
                    if near(src, (i, j)) and any(near((i, j), d) for d in dsts)
                ]
                lhs = jnp.concatenate([c.get(left, src, m) for m in mids], axis=1)
                rhs = jnp.concatenate(
                    [
                        jnp.concatenate([c.get(right, m, d) if near(m, d) else zero for d in dsts], axis=1)
                        for m in mids
                    ],
                    axis=0,
                )
                total = jnp.dot(lhs, rhs, precision=lax.Precision.HIGH, preferred_element_type=jnp.float32)
                for n, d in enumerate(dsts):
                    value = total[:, n * block : (n + 1) * block]
                    emit(c, src, d, c.keep(pat, src, d) * value)

        corners(body)

    def mirror(table):
        def body(c):
            for src, dst in (((0, 1), (1, 1)), ((1, 0), (1, 1)), ((1, 0), (0, 1))):
                table[c.index(dst, src)] = c.get(table, src, dst).T

        corners(body)
        for p, q in (((0, 1), (0, 2)), ((3, 1), (3, 2)), ((1, 0), (2, 0)), ((1, 3), (2, 3))):
            k = offset(q[0] - p[0], q[1] - p[1])
            table[q[0] * 4 + q[1], 8 - k] = table[p[0] * 4 + p[1], k].T

    def mask(c):
        for i in (-1, 0, 1):
            for j in (-1, 0, 1):
                here = (0, 0)
                a, b, k = c.at(here, (i, j))
                value = c.keep(pat, here, (i, j)) * start[a - 1, b - 1, k]
                x0[c.index(here, (i, j))] = value
                if max(i, j) == 1:
                    x0[c.index((i, j), here)] = value.T

    def square(c, src, dst, value):
        s0[c.index(src, dst)] = value
        if max(dst) == 1:
            s0[c.index(dst, src)] = value.T

    def advance(c, src, dst, value):
        x1[c.index(src, dst)] = 1.5 * c.get(x0, src, dst) - 0.5 * value

    def square_again(c, src, dst, value):
        s1[c.index(src, dst)] = value

    def finish(c, src, dst, value):
        a, b, k = c.at(src, dst)
        out[a - 1, b - 1, k] = 1.5 * c.get(x1, src, dst) - 0.5 * value

    corners(mask)
    pl.semaphore_wait(barrier, len(SIDES))
    begin(0, 0)
    begin(0, 1)
    product(x0, x0, INNER, square)
    begin(1, 0)
    pass_on(0)
    settle(0)
    mirror(x0)
    product(x0, x0, OUTER, square)
    begin(1, 1)
    product(x0, s0, INNER, advance)
    begin(2, 0)
    pass_on(1)
    product(x0, s0, RING, advance)
    settle(1)
    mirror(s0)
    product(x0, s0, OUTER, advance)
    begin(2, 1)
    product(x1, x1, INNER, square_again)
    begin(3, 0)
    pass_on(2)
    settle(2)
    product(x1, x1, OUTER, square_again)
    product(x1, x1, RING, square_again)
    begin(3, 1)
    product(x1, s1, INNER, finish)
    pass_on(3)
    settle(3)
    product(x1, s1, OUTER, finish)
    for phase in range(4):
        for group in range(3):
            for c in copies(phase, group):
                c.wait_send()


def solution(mesh):
    rows, cols = mesh.shape["row"], mesh.shape["col"]

    def step(pattern, start):
        block = start.shape[-1]
        return pl.pallas_call(
            functools.partial(kernel, rows, cols),
            out_shape=jax.ShapeDtypeStruct(start.shape, jnp.float32),
            in_specs=[pl.BlockSpec(memory_space=pltpu.SMEM), pl.BlockSpec(memory_space=pltpu.VMEM)],
            out_specs=pl.BlockSpec(memory_space=pltpu.VMEM),
            scratch_shapes=[pltpu.VMEM((16, 9, block, block), jnp.float32)] * 4
            + [pltpu.SemaphoreType.DMA((4, 4, 14))] * 2,
            compiler_params=pltpu.CompilerParams(
                collective_id=0, has_side_effects=True, vmem_limit_bytes=56 * 1024 * 1024
            ),
            cost_estimate=pl.CostEstimate(
                flops=2 * 976 * block**3, bytes_accessed=2 * start.size * 4, transcendentals=0
            ),
        )(pattern, start)

    return jax.shard_map(
        step,
        mesh=mesh,
        in_specs=(P("row", "col", None), P("row", "col", None, None, None)),
        out_specs=P("row", "col", None, None, None),
        check_vma=False,
    )
```

profile of v0, /device:TPU:1, one launch (start us, length us, event | category | flops | bytes accessed | tf_op | source)
XLA Modules:
  0.0 76.6 jit_solution(17728244728368397177)
XLA Ops:
  0.0 73.2 %shard_map.28 = f32[2,2,9,128,128]{4,3,2,1,0:T(8,128)} custom-call(s32[2,2,9]{2,1,0:T(2,128)} %pat.1, f32[2,2,9,128,128]{4,3,2,1,0:T(8,128)} %start.1), custom_call_target="tpu_custom_call" | custom-call | flops 4093640704 | bytes 4718592 | tf_op jit(solution)/shard_map/pallas_call | solution.py:242
  73.2 3.3 %copy.4 = f32[2,2,9,128,128]{4,3,2,1,0:T(8,128)} copy(f32[2,2,9,128,128]{4,3,2,1,0:T(8,128)} %shard_map.28) | data formatting | bytes 4718592
where the time goes:
time: 77.6 us; the launch traced here: 76.6 us
  Pallas kernels  73.2 us (94%)
  local copies, waits for them, and re-layouts  3.32 us (4%)
    pallas_call x1, Pallas kernels, step(): pl.pallas_call(functools.partial(kernel, rows, cols), out_shape=jax.Shape...  73.2 us
    unnamed x1, local copies, waits for them, and re-layouts  3.32 us

commit v1 on v0

v1 whole, which is shorter than its diff:
```python
import functools

import jax
import jax.numpy as jnp
from jax import lax
from jax.experimental import pallas as pl
from jax.experimental.pallas import tpu as pltpu
from jax.sharding import PartitionSpec as P

MESH = pl.DeviceIdType.MESH
INNER = (((0, 0), ((0, 0), (0, -1))), ((0, 0), ((-1, 0), (-1, -1))))
OUTER = (
    ((0, 0), ((1, 1), (1, 0))),
    ((0, 0), ((0, 1), (-1, 1))),
    ((0, 0), ((1, -1),)),
)
RING = (
    ((1, 0), ((0, 0), (0, -1))),
    ((0, 1), ((0, 0), (-1, 0))),
    ((1, 1), ((0, 0),)),
)
FLIPS = (((0, 1), (1, 1)), ((1, 0), (1, 1)), ((1, 0), (0, 1)))
OUTSIDE = ((1, 1), (1, 0), (1, -1), (0, 1), (-1, 1))
KINDS = {
    "x_self": (1, (0, 0), (0, 0), 0),
    "x_side": (1, (0, 0), (-1, 0), 2),
    "x_pair": (1, (0, 0), (1, 0), 4),
    "x_back": (1, (1, 0), (0, 0), 6),
    "y_self": (0, (0, 0), (0, 0), 0),
    "y_side": (0, (0, 0), (0, -1), 2),
    "y_pair": (0, (0, 0), (0, 1), 4),
    "y_diag": (0, (0, 0), (1, 1), 6),
    "y_back": (0, (0, 1), (0, 0), 8),
    "y_gaid": (0, (1, 1), (0, 0), 10),
    "relay": (0, (0, 1), (0, 1), 12),
}
FIRST = ("x_self", "y_self", "x_side", "y_side")
PAIRS = ("x_pair", "y_pair", "y_diag")
BACKS = ("x_back", "y_back", "y_gaid")


def near(p, q):
    return abs(p[0] - q[0]) <= 1 and abs(p[1] - q[1]) <= 1


class Corner:
    def __init__(self, n):
        self.n = n
        self.a, self.b = 1 + n // 2, 1 + lax.rem(n, 2)
        self.down, self.across = 2 * self.a - 3, 2 * self.b - 3

    def at(self, src, dst):
        i = self.a + src[0] * self.down
        j = self.b + src[1] * self.across
        k = 4 + 3 * (dst[0] - src[0]) * self.down + (dst[1] - src[1]) * self.across
        return i, j, k

    def index(self, src, dst):
        i, j, k = self.at(src, dst)
        return i * 4 + j, k

    def get(self, ref, src, dst):
        return ref[self.index(src, dst)]

    def keep(self, pat, src, dst):
        if max(src) == 1:
            src, dst = dst, src
        i, j, k = self.at(src, dst)
        return pat[i - 1, j - 1, k].astype(jnp.float32)


def kernel(rows, cols, pat, start, out, tile, x0, s0, x1, s1, send_sem, recv_sem, load_sem, store_sem):
    row, col = lax.axis_index("row"), lax.axis_index("col")
    block = start.shape[-1]
    tables = (x0, s0, x1, s1)

    def device(side):
        return (lax.rem(row + side[0] + rows, rows), lax.rem(col + side[1] + cols, cols))

    def load(c):
        return pltpu.make_async_copy(start.at[c.a - 1, c.b - 1], tile.at[c.n], load_sem.at[c.n])

    def store(c):
        return pltpu.make_async_copy(tile.at[c.n], out.at[c.a - 1, c.b - 1], store_sem.at[c.n])

    def corners(body):
        def step(n, carry):
            body(Corner(n))
            return carry

        lax.fori_loop(0, 4, step, 0)

    def guarded(phase, kind, c, action):
        if phase < 2 and kind in ("x_side", "y_side"):
            pl.when((c.a if kind == "x_side" else c.b) == 1)(action)
        else:
            action()

    def outgoing(phase, kind, c):
        axis, src, dst, slot = KINDS[kind]
        site, k = c.index(src, dst)
        if axis == 1:
            there, to, d, slot = site - 2 * c.across, device((0, c.across)), 2 - c.b, slot + c.a - 1
        else:
            there, to, d, slot = site - 8 * c.down, device((c.down, 0)), 4 - c.a, slot + c.b - 1
        return pltpu.make_async_remote_copy(
            src_ref=tables[phase].at[site, k],
            dst_ref=tables[phase].at[there, k],
            send_sem=send_sem.at[phase, d, slot],
            recv_sem=recv_sem.at[phase, d, slot],
            device_id=to,
            device_id_type=MESH,
        )

    def incoming(phase, kind, c):
        axis, src, dst, slot = KINDS[kind]
        if axis == 1:
            src, dst = (src[0], 1 - src[1]), (dst[0], 1 - dst[1])
            d, slot = c.b - 1, slot + c.a - 1
        else:
            src, dst = (1 - src[0], src[1]), (1 - dst[0], dst[1])
            d, slot = c.a + 1, slot + c.b - 1
        landing = tables[phase].at[c.index(src, dst)]
        return pltpu.make_async_remote_copy(
            src_ref=landing,
            dst_ref=landing,
            send_sem=send_sem.at[phase, d, slot],
            recv_sem=recv_sem.at[phase, d, slot],
            device_id=device((0, c.across) if axis == 1 else (c.down, 0)),
            device_id_type=MESH,
        )

    def send(phase, kinds, c):
        for kind in kinds:
            guarded(phase, kind, c, lambda kind=kind: outgoing(phase, kind, c).start())

    def receive(phase, kinds, c):
        for kind in kinds:
            guarded(phase, kind, c, lambda kind=kind: incoming(phase, kind, c).wait_recv())

    def pass_on(phase):
        def body(c):
            receive(phase, ("x_self",), c)
            send(phase, ("relay",), c)

        corners(body)

    def settle(phase):
        corners(lambda c: receive(phase, FIRST[1:] + (() if phase < 2 else BACKS), c))

    def product(c, left, right, groups, emit, flips=()):
        zero = jnp.zeros((block, block), jnp.float32)
        flipped = {}
        for src, dst in flips:
            flipped[dst, src] = c.get(right, src, dst).T
            right[c.index(dst, src)] = flipped[dst, src]

        def piece(m, d):
            if not near(m, d):
                return zero
            return flipped[m, d] if (m, d) in flipped else c.get(right, m, d)

        for src, dsts in groups:
            mids = [
                (i, j)
                for i in (-1, 0, 1)
                for j in (-1, 0, 1)
                if near(src, (i, j)) and any(near((i, j), d) for d in dsts)
            ]
            lhs = jnp.concatenate([c.get(left, src, m) for m in mids], axis=1)
            rhs = jnp.concatenate([jnp.concatenate([piece(m, d) for d in dsts], axis=1) for m in mids], axis=0)
            total = jnp.dot(lhs, rhs, precision=lax.Precision.HIGH, preferred_element_type=jnp.float32)
            for n, d in enumerate(dsts):
                emit(c, src, d, c.keep(pat, src, d) * total[:, n * block : (n + 1) * block])

    def mirror(table):
        for p, q in (((0, 1), (0, 2)), ((3, 1), (3, 2)), ((1, 0), (2, 0)), ((1, 3), (2, 3))):
            k = 4 + 3 * (q[0] - p[0]) + q[1] - p[1]
            table[q[0] * 4 + q[1], 8 - k] = table[p[0] * 4 + p[1], k].T

    def fold(table):
        def body(c):
            for dst in OUTSIDE:
                table[c.index(dst, (0, 0))] = c.get(table, (0, 0), dst).T

        corners(body)

    def square(c, src, dst, value):
        s0[c.index(src, dst)] = value

    def advance(c, src, dst, value):
        x1[c.index(src, dst)] = 1.5 * c.get(x0, src, dst) - 0.5 * value

    def square_again(c, src, dst, value):
        s1[c.index(src, dst)] = value

    def finish(c, src, dst, value):
        tile[c.n, c.at(src, dst)[2]] = 1.5 * c.get(x1, src, dst) - 0.5 * value

    def mask(c):
        load(c).wait()
        for k in range(9):
            x0[c.a * 4 + c.b, k] = pat[c.a - 1, c.b - 1, k].astype(jnp.float32) * tile[c.n, k]
        send(0, FIRST + PAIRS, c)

    def square_inside(c):
        product(c, x0, x0, INNER, square)
        send(1, FIRST, c)

    def square_outside(c):
        receive(0, PAIRS + ("relay",), c)
        product(c, x0, x0, OUTER, square, FLIPS)
        send(1, PAIRS, c)

    def advance_inside(c):
        product(c, x0, s0, INNER, advance)
        send(2, FIRST, c)

    def advance_ring(c):
        product(c, x0, s0, RING, advance)
        send(2, BACKS, c)

    def advance_outside(c):
        receive(1, PAIRS + ("relay",), c)
        product(c, x0, s0, OUTER, advance, FLIPS)
        send(2, PAIRS, c)

    def square_again_inside(c):
        product(c, x1, x1, INNER, square_again)
        send(3, FIRST, c)

    def square_again_outside(c):
        receive(2, PAIRS + ("relay",), c)
        product(c, x1, x1, OUTER, square_again)
        send(3, PAIRS, c)
        product(c, x1, x1, RING, square_again)
        send(3, BACKS, c)

    def finish_outside(c):
        receive(3, PAIRS + ("relay",), c)
        product(c, x1, s1, OUTER, finish)
        store(c).start()

    corners(lambda c: load(c).start())
    barrier = pltpu.get_barrier_semaphore()
    sides = ((0, 1), (0, -1), (1, 0), (-1, 0))
    for side in sides:
        pl.semaphore_signal(barrier, inc=1, device_id=device(side), device_id_type=MESH)
    pl.semaphore_wait(barrier, len(sides))
    corners(mask)
    fold(x0)
    corners(square_inside)
    pass_on(0)
    settle(0)
    mirror(x0)
    corners(square_outside)
    pass_on(1)
    fold(s0)
    corners(advance_inside)
    corners(advance_ring)
    settle(1)
    mirror(s0)
    corners(advance_outside)
    pass_on(2)
    corners(square_again_inside)
    settle(2)
    corners(square_again_outside)
    pass_on(3)
    corners(lambda c: product(c, x1, s1, INNER, finish))
    settle(3)
    corners(finish_outside)

    def drain(c):
        store(c).wait()
        for phase in range(4):
            for kind in KINDS:
                if phase >= 2 or kind not in BACKS:
                    guarded(phase, kind, c, lambda p=phase, k=kind: outgoing(p, k, c).wait_send())

    corners(drain)


def solution(mesh):
    rows, cols = mesh.shape["row"], mesh.shape["col"]

    def step(pattern, start):
        block = start.shape[-1]
        return pl.pallas_call(
            functools.partial(kernel, rows, cols),
            out_shape=jax.ShapeDtypeStruct(start.shape, jnp.float32),
            in_specs=[pl.BlockSpec(memory_space=pltpu.SMEM), pl.BlockSpec(memory_space=pl.ANY)],
            out_specs=pl.BlockSpec(memory_space=pl.ANY),
            scratch_shapes=[pltpu.VMEM((4, 9, block, block), jnp.float32)]
            + [pltpu.VMEM((16, 9, block, block), jnp.float32)] * 4
            + [pltpu.SemaphoreType.DMA((4, 4, 14))] * 2
            + [pltpu.SemaphoreType.DMA((4,))] * 2,
            compiler_params=pltpu.CompilerParams(
                collective_id=0, has_side_effects=True, vmem_limit_bytes=56 * 1024 * 1024
            ),
            cost_estimate=pl.CostEstimate(
                flops=2 * 976 * block**3, bytes_accessed=2 * start.size * 4, transcendentals=0
            ),
        )(pattern, start)

    return jax.shard_map(
        step,
        mesh=mesh,
        in_specs=(P("row", "col", None), P("row", "col", None, None, None)),
        out_specs=P("row", "col", None, None, None),
        check_vma=False,
    )
```

time: 77.6 us -> 61.4 us (0.79)
  Pallas kernels: 73.2 us -> 57.1 us
    pallas_call x1, Pallas kernels: 73.2 us -> 57.1 us  [step(): pl.pallas_call(functools.partial(kernel, rows, cols), out_shape=jax.Shape...]
where the time goes in v1:
time: 61.4 us; the launch traced here: 60.4 us
  Pallas kernels  57.1 us (93%)
  local copies, waits for them, and re-layouts  3.32 us (5%)
    pallas_call x1, Pallas kernels, step(): pl.pallas_call(functools.partial(kernel, rows, cols), out_shape=jax.Shape...  57.1 us
    unnamed x1, local copies, waits for them, and re-layouts  3.32 us

profile of v1, /device:TPU:1, one launch (start us, length us, event | category | flops | bytes accessed | tf_op | source)
XLA Modules:
  0.0 60.4 jit_solution(7815155548053155450)
XLA Ops:
  0.0 57.1 %shard_map.28 = f32[2,2,9,128,128]{4,3,2,1,0:T(8,128)} custom-call(s32[2,2,9]{2,1,0:T(2,128)} %pat.1, f32[2,2,9,128,128]{4,3,2,1,0:T(8,128)} %start.1), custom_call_target="tpu_custom_call" | custom-call | flops 4093640704 | bytes 4718592 | tf_op jit(solution)/shard_map/pallas_call | solution.py:288
  57.1 3.3 %copy.4 = f32[2,2,9,128,128]{4,3,2,1,0:T(8,128)} copy(f32[2,2,9,128,128]{4,3,2,1,0:T(8,128)} %shard_map.28) | data formatting | bytes 4718592

commit v2 on v1

--- a/solution.py
+++ b/solution.py
@@ -33,6 +33,7 @@
     "y_back": (0, (0, 1), (0, 0), 8),
     "y_gaid": (0, (1, 1), (0, 0), 10),
     "relay": (0, (0, 1), (0, 1), 12),
+    "hop": (0, (0, 1), (1, 1), 14),
 }
 FIRST = ("x_self", "y_self", "x_side", "y_side")
 PAIRS = ("x_pair", "y_pair", "y_diag")
@@ -44,9 +45,12 @@
 
 
 class Corner:
-    def __init__(self, n):
-        self.n = n
-        self.a, self.b = 1 + n // 2, 1 + lax.rem(n, 2)
+    def __init__(self, step, core):
+        self.step = step
+        half = step // 2
+        self.inner = half == 1
+        self.a, self.b = 1 + half + core * (1 - 2 * half), 1 + lax.rem(step, 2)
+        self.n = 2 * self.a + self.b - 3
         self.down, self.across = 2 * self.a - 3, 2 * self.b - 3
 
     def at(self, src, dst):
@@ -69,7 +73,7 @@
         return pat[i - 1, j - 1, k].astype(jnp.float32)
 
 
-def kernel(rows, cols, pat, start, out, tile, x0, s0, x1, s1, send_sem, recv_sem, load_sem, store_sem):
+def kernel(rows, cols, pat, start, out, tile, x0, s0, x1, s1, send_sem, recv_sem, load_sem):
     row, col = lax.axis_index("row"), lax.axis_index("col")
     block = start.shape[-1]
     tables = (x0, s0, x1, s1)
@@ -80,12 +84,9 @@
     def load(c):
         return pltpu.make_async_copy(start.at[c.a - 1, c.b - 1], tile.at[c.n], load_sem.at[c.n])
 
-    def store(c):
-        return pltpu.make_async_copy(tile.at[c.n], out.at[c.a - 1, c.b - 1], store_sem.at[c.n])
-
     def corners(body):
         def step(n, carry):
-            body(Corner(n))
+            body(Corner(n, lax.rem(row, 2)))
             return carry
 
         lax.fori_loop(0, 4, step, 0)
@@ -93,6 +94,10 @@
     def guarded(phase, kind, c, action):
         if phase < 2 and kind in ("x_side", "y_side"):
             pl.when((c.a if kind == "x_side" else c.b) == 1)(action)
+        elif kind == "x_back":
+            pl.when(jnp.logical_not(c.inner))(action)
+        elif kind == "hop":
+            pl.when(c.inner)(action)
         else:
             action()
 
@@ -145,6 +150,17 @@
 
         corners(body)
 
+    def collect(phase, c):
+        @pl.when(c.step == 1)
+        def _():
+            for step in (2, 3):
+                other = Corner(step, lax.rem(row, 2))
+                receive(phase, ("x_pair",), other)
+                send(phase, ("hop",), other)
+
+        pl.when(jnp.logical_not(c.inner))(lambda: receive(phase, ("x_pair",), c))
+        receive(phase, PAIRS[1:] + ("hop", "relay"), c)
+
     def settle(phase):
         corners(lambda c: receive(phase, FIRST[1:] + (() if phase < 2 else BACKS), c))
 
@@ -178,15 +194,14 @@
             k = 4 + 3 * (q[0] - p[0]) + q[1] - p[1]
             table[q[0] * 4 + q[1], 8 - k] = table[p[0] * 4 + p[1], k].T
 
-    def fold(table):
-        def body(c):
-            for dst in OUTSIDE:
-                table[c.index(dst, (0, 0))] = c.get(table, (0, 0), dst).T
-
-        corners(body)
+    def fold(c):
+        for dst in OUTSIDE:
+            x0[c.index(dst, (0, 0))] = c.get(x0, (0, 0), dst).T
 
     def square(c, src, dst, value):
         s0[c.index(src, dst)] = value
+        if max(dst) == 1:
+            s0[c.index(dst, src)] = value.T
 
     def advance(c, src, dst, value):
         x1[c.index(src, dst)] = 1.5 * c.get(x0, src, dst) - 0.5 * value
@@ -195,7 +210,7 @@
         s1[c.index(src, dst)] = value
 
     def finish(c, src, dst, value):
-        tile[c.n, c.at(src, dst)[2]] = 1.5 * c.get(x1, src, dst) - 0.5 * value
+        out[c.a - 1, c.b - 1, c.at(src, dst)[2]] = 1.5 * c.get(x1, src, dst) - 0.5 * value
 
     def mask(c):
         load(c).wait()
@@ -230,16 +245,15 @@
         send(3, FIRST, c)
 
     def square_again_outside(c):
-        receive(2, PAIRS + ("relay",), c)
+        collect(2, c)
         product(c, x1, x1, OUTER, square_again)
         send(3, PAIRS, c)
         product(c, x1, x1, RING, square_again)
         send(3, BACKS, c)
 
     def finish_outside(c):
-        receive(3, PAIRS + ("relay",), c)
+        collect(3, c)
         product(c, x1, s1, OUTER, finish)
-        store(c).start()
 
     corners(lambda c: load(c).start())
     barrier = pltpu.get_barrier_semaphore()
@@ -248,14 +262,13 @@
         pl.semaphore_signal(barrier, inc=1, device_id=device(side), device_id_type=MESH)
     pl.semaphore_wait(barrier, len(sides))
     corners(mask)
-    fold(x0)
+    corners(fold)
     corners(square_inside)
     pass_on(0)
     settle(0)
     mirror(x0)
     corners(square_outside)
     pass_on(1)
-    fold(s0)
     corners(advance_inside)
     corners(advance_ring)
     settle(1)
@@ -271,10 +284,9 @@
     corners(finish_outside)
 
     def drain(c):
-        store(c).wait()
         for phase in range(4):
             for kind in KINDS:
-                if phase >= 2 or kind not in BACKS:
+                if phase >= 2 or kind not in BACKS + ("hop",):
                     guarded(phase, kind, c, lambda p=phase, k=kind: outgoing(p, k, c).wait_send())
 
     corners(drain)
@@ -287,15 +299,15 @@
         block = start.shape[-1]
         return pl.pallas_call(
             functools.partial(kernel, rows, cols),
-            out_shape=jax.ShapeDtypeStruct(start.shape, jnp.float32),
+            out_shape=pltpu.VMEM(start.shape, jnp.float32),
             in_specs=[pl.BlockSpec(memory_space=pltpu.SMEM), pl.BlockSpec(memory_space=pl.ANY)],
-            out_specs=pl.BlockSpec(memory_space=pl.ANY),
+            out_specs=pl.BlockSpec(memory_space=pltpu.VMEM),
             scratch_shapes=[pltpu.VMEM((4, 9, block, block), jnp.float32)]
             + [pltpu.VMEM((16, 9, block, block), jnp.float32)] * 4
-            + [pltpu.SemaphoreType.DMA((4, 4, 14))] * 2
-            + [pltpu.SemaphoreType.DMA((4,))] * 2,
+            + [pltpu.SemaphoreType.DMA((4, 4, 16))] * 2
+            + [pltpu.SemaphoreType.DMA((4,))],
             compiler_params=pltpu.CompilerParams(
-                collective_id=0, has_side_effects=True, vmem_limit_bytes=56 * 1024 * 1024
+                collective_id=0, has_side_effects=True, vmem_limit_bytes=60 * 1024 * 1024
             ),
             cost_estimate=pl.CostEstimate(
                 flops=2 * 976 * block**3, bytes_accessed=2 * start.size * 4, transcendentals=0

time: 61.4 us -> 56 us (0.912); the launches traced: 60.4 us -> 55.9 us
  Pallas kernels: 57.1 us -> 54.4 us
  local copies, waits for them, and re-layouts: 3.32 us -> 1.41 us
    pallas_call x1, Pallas kernels: 57.1 us -> 54.4 us  [step(): pl.pallas_call(functools.partial(kernel, rows, cols), out_shape=pltpu.VME...]
    unnamed x1, local copies, waits for them, and re-layouts: 3.32 us -> 1.41 us
where the time goes in v2:
time: 56 us; the launch traced here: 55.9 us
  Pallas kernels  54.4 us (97%)
  local copies, waits for them, and re-layouts  1.41 us (3%)
    pallas_call x1, Pallas kernels, step(): pl.pallas_call(functools.partial(kernel, rows, cols), out_shape=pltpu.VME...  54.4 us
    unnamed x1, local copies, waits for them, and re-layouts  1.41 us

profile of v2, /device:TPU:1, one launch (start us, length us, event | category | flops | bytes accessed | tf_op | source)
XLA Modules:
  0.0 55.9 jit_solution(10470960291031674907)
XLA Ops:
  0.0 54.4 %shard_map.28 = f32[2,2,9,128,128]{4,3,2,1,0:T(8,128)S(1)} custom-call(s32[2,2,9]{2,1,0:T(2,128)} %pat.1, f32[2,2,9,128,128]{4,3,2,1,0:T(8,128)} %start.1), custom_call_target="tpu_custom_call" | custom-call | flops 4093640704 | bytes 4718592 | tf_op jit(solution)/shard_map/pallas_call | solution.py:300
  54.5 1.4 %copy.4 = f32[2,2,9,128,128]{4,3,2,1,0:T(8,128)} copy(f32[2,2,9,128,128]{4,3,2,1,0:T(8,128)S(1)} %shard_map.28) | data formatting | bytes 4718592

commit v3 on v2

--- a/solution.py
+++ b/solution.py
@@ -20,6 +20,7 @@
     ((1, 1), ((0, 0),)),
 )
 FLIPS = (((0, 1), (1, 1)), ((1, 0), (1, 1)), ((1, 0), (0, 1)))
+LATE = ((0, 1), (1, 0), (1, 1))
 OUTSIDE = ((1, 1), (1, 0), (1, -1), (0, 1), (-1, 1))
 KINDS = {
     "x_self": (1, (0, 0), (0, 0), 0),
@@ -143,12 +144,11 @@
         for kind in kinds:
             guarded(phase, kind, c, lambda kind=kind: incoming(phase, kind, c).wait_recv())
 
-    def pass_on(phase):
-        def body(c):
+    def pass_on(phase, steps=(0, 1, 2, 3)):
+        for step in steps:
+            c = Corner(step, lax.rem(row, 2))
             receive(phase, ("x_self",), c)
             send(phase, ("relay",), c)
-
-        corners(body)
 
     def collect(phase, c):
         @pl.when(c.step == 1)
@@ -162,9 +162,17 @@
         receive(phase, PAIRS[1:] + ("hop", "relay"), c)
 
     def settle(phase):
-        corners(lambda c: receive(phase, FIRST[1:] + (() if phase < 2 else BACKS), c))
-
-    def product(c, left, right, groups, emit, flips=()):
+        corners(lambda c: receive(phase, FIRST[1:], c))
+
+    def sent(phases, kinds):
+        def body(c):
+            for phase in phases:
+                for kind in kinds:
+                    guarded(phase, kind, c, lambda p=phase, k=kind: outgoing(p, k, c).wait_send())
+
+        corners(body)
+
+    def product(c, left, right, groups, emit, flips=(), leave=(), only=None):
         zero = jnp.zeros((block, block), jnp.float32)
         flipped = {}
         for src, dst in flips:
@@ -182,6 +190,7 @@
                 for i in (-1, 0, 1)
                 for j in (-1, 0, 1)
                 if near(src, (i, j)) and any(near((i, j), d) for d in dsts)
+                if (i, j) not in leave and (only is None or (i, j) in only)
             ]
             lhs = jnp.concatenate([c.get(left, src, m) for m in mids], axis=1)
             rhs = jnp.concatenate([jnp.concatenate([piece(m, d) for d in dsts], axis=1) for m in mids], axis=0)
@@ -212,6 +221,9 @@
     def finish(c, src, dst, value):
         out[c.a - 1, c.b - 1, c.at(src, dst)[2]] = 1.5 * c.get(x1, src, dst) - 0.5 * value
 
+    def complete(c, src, dst, value):
+        out[c.a - 1, c.b - 1, c.at(src, dst)[2]] -= 0.5 * value
+
     def mask(c):
         load(c).wait()
         for k in range(9):
@@ -236,6 +248,7 @@
         send(2, BACKS, c)
 
     def advance_outside(c):
+        pl.when(c.step == 2)(lambda: pass_on(2, (0, 1)))
         receive(1, PAIRS + ("relay",), c)
         product(c, x0, s0, OUTER, advance, FLIPS)
         send(2, PAIRS, c)
@@ -245,15 +258,22 @@
         send(3, FIRST, c)
 
     def square_again_outside(c):
+        pl.when(c.step == 3)(lambda: pass_on(3, (0, 1)))
+        receive(2, BACKS, c)
         collect(2, c)
         product(c, x1, x1, OUTER, square_again)
         send(3, PAIRS, c)
         product(c, x1, x1, RING, square_again)
         send(3, BACKS, c)
 
+    def finish_early(c):
+        product(c, x1, s1, OUTER[2:], finish)
+        product(c, x1, s1, OUTER[:2], finish, leave=LATE)
+
     def finish_outside(c):
+        receive(3, BACKS, c)
         collect(3, c)
-        product(c, x1, s1, OUTER, finish)
+        product(c, x1, s1, OUTER[:2], complete, only=LATE)
 
     corners(lambda c: load(c).start())
     barrier = pltpu.get_barrier_semaphore()
@@ -274,22 +294,19 @@
     settle(1)
     mirror(s0)
     corners(advance_outside)
-    pass_on(2)
+    pass_on(2, (2, 3))
     corners(square_again_inside)
     settle(2)
     corners(square_again_outside)
-    pass_on(3)
+    pass_on(3, (2, 3))
     corners(lambda c: product(c, x1, s1, INNER, finish))
+    sent((0, 1), FIRST + PAIRS + ("relay",))
+    sent((2,), FIRST + BACKS + PAIRS + ("hop", "relay"))
     settle(3)
+    corners(finish_early)
+    sent((3,), FIRST + BACKS)
     corners(finish_outside)
-
-    def drain(c):
-        for phase in range(4):
-            for kind in KINDS:
-                if phase >= 2 or kind not in BACKS + ("hop",):
-                    guarded(phase, kind, c, lambda p=phase, k=kind: outgoing(p, k, c).wait_send())
-
-    corners(drain)
+    sent((3,), PAIRS + ("hop", "relay"))
 
 
 def solution(mesh):

time: 56 us -> 55.7 us (level)
  no operation moved by 1% of the time
where the time goes in v3:
time: 55.7 us; the launch traced here: 55.6 us
  Pallas kernels  54.1 us (97%)
  local copies, waits for them, and re-layouts  1.41 us (3%)
    pallas_call x1, Pallas kernels, step(): pl.pallas_call(functools.partial(kernel, rows, cols), out_shape=pltpu.VME...  54.1 us
    unnamed x1, local copies, waits for them, and re-layouts  1.41 us

profile of v3, /device:TPU:1, one launch (start us, length us, event | category | flops | bytes accessed | tf_op | source)
XLA Modules:
  0.0 55.6 jit_solution(573775947586183810)
XLA Ops:
  0.0 54.1 %shard_map.28 = f32[2,2,9,128,128]{4,3,2,1,0:T(8,128)S(1)} custom-call(s32[2,2,9]{2,1,0:T(2,128)} %pat.1, f32[2,2,9,128,128]{4,3,2,1,0:T(8,128)} %start.1), custom_call_target="tpu_custom_call" | custom-call | flops 4093640704 | bytes 4718592 | tf_op jit(solution)/shard_map/pallas_call | solution.py:317
  54.1 1.4 %copy.4 = f32[2,2,9,128,128]{4,3,2,1,0:T(8,128)} copy(f32[2,2,9,128,128]{4,3,2,1,0:T(8,128)S(1)} %shard_map.28) | data formatting | bytes 4718592

commit v4 on v3

--- a/solution.py
+++ b/solution.py
@@ -261,8 +261,10 @@
         pl.when(c.step == 3)(lambda: pass_on(3, (0, 1)))
         receive(2, BACKS, c)
         collect(2, c)
-        product(c, x1, x1, OUTER, square_again)
-        send(3, PAIRS, c)
+        product(c, x1, x1, OUTER[:1], square_again)
+        send(3, ("x_pair", "y_diag"), c)
+        product(c, x1, x1, OUTER[1:2], square_again)
+        send(3, ("y_pair",), c)
         product(c, x1, x1, RING, square_again)
         send(3, BACKS, c)
 
@@ -299,6 +301,7 @@
     settle(2)
     corners(square_again_outside)
     pass_on(3, (2, 3))
+    corners(lambda c: product(c, x1, x1, OUTER[2:], square_again))
     corners(lambda c: product(c, x1, s1, INNER, finish))
     sent((0, 1), FIRST + PAIRS + ("relay",))
     sent((2,), FIRST + BACKS + PAIRS + ("hop", "relay"))

time: 55.7 us -> 57.7 us (1.036)
  Pallas kernels: 54.1 us -> 56.1 us
    pallas_call x1, Pallas kernels: 54.1 us -> 56.1 us  [step(): pl.pallas_call(functools.partial(kernel, rows, cols), out_shape=pltpu.VME...]
where the time goes in v4:
time: 57.7 us; the launch traced here: 57.6 us
  Pallas kernels  56.1 us (97%)
  local copies, waits for them, and re-layouts  1.41 us (2%)
    pallas_call x1, Pallas kernels, step(): pl.pallas_call(functools.partial(kernel, rows, cols), out_shape=pltpu.VME...  56.1 us
    unnamed x1, local copies, waits for them, and re-layouts  1.41 us

profile of v4, /device:TPU:1, one launch (start us, length us, event | category | flops | bytes accessed | tf_op | source)
XLA Modules:
  0.0 57.6 jit_solution(3024961152084314021)
XLA Ops:
  0.0 56.1 %shard_map.28 = f32[2,2,9,128,128]{4,3,2,1,0:T(8,128)S(1)} custom-call(s32[2,2,9]{2,1,0:T(2,128)} %pat.1, f32[2,2,9,128,128]{4,3,2,1,0:T(8,128)} %start.1), custom_call_target="tpu_custom_call" | custom-call | flops 4093640704 | bytes 4718592 | tf_op jit(solution)/shard_map/pallas_call | solution.py:320
  56.2 1.4 %copy.4 = f32[2,2,9,128,128]{4,3,2,1,0:T(8,128)} copy(f32[2,2,9,128,128]{4,3,2,1,0:T(8,128)S(1)} %shard_map.28) | data formatting | bytes 4718592
